TPU v7x, 32 devices: a whole 2x2x4 slice. The times are simulated.
32 devices in a mesh: frame: 16 (over z, y, x), pix: 2 (over core).
Axes of the slice: x: 2, y: 2, z: 4, core: 2. Of those that a mesh axis runs over, the one named last changes fastest.
Arguments:
- frames: bfloat16 [1024, 32768], P('frame', 'pix'), as said below
- cycle_map: int32 [32768], P('pix'), may hold values from -1 to 15, as said below
Outputs:
- correlation: bfloat16 [16, 1024, 1024], P('frame', 'pix')
Inputs may be any that keep to these rules, and one draw needn't show every extreme that they name: `frames`: every entry is positive. `cycle_map`: pixels come in aligned blocks of 128; every pixel of a block is either -1 or one common cycle, and the first pixel of a block that holds a cycle belongs to it. Within each sector (aligned blocks of 16384 pixels, one a pix group) every cycle holds at least one and at most 8 blocks, and every cycle holds exactly 1024 pixels in some sector.
All inputs are finite; a program needn't handle non-finite values.
Results may differ from a plain program's by a relative error of at most 0.012.
Values may be sent and summed in bfloat16 or wider, within the bound.
No kernel may reach another device: no remote copies, remote signals or barrier semaphores. Data moves between devices by JAX's collectives and lax.ppermute only.
A program may use at most 64 MiB of HBM per device.

v0:
```python
import functools

import jax
import jax.numpy as jnp
from jax import lax
from jax.experimental import pallas as pl
from jax.experimental.pallas import tpu as pltpu
from jax.sharding import PartitionSpec as P

BLOCK = 128
HALF_WIN = 2
PAD = 8
TILE = 256
CHUNK = 128
ONES = 16
VMEM_BYTES = 32 * 1024 * 1024
LIST, COUNT, PIXELS = 0, 1, 2
MERGED = 2
BITS = 16
SWAP = [(0, 1), (1, 0)]
WHOLE = pl.BlockSpec(memory_space=pltpu.VMEM)
ANYWHERE = pl.BlockSpec(memory_space=pl.ANY)


def call(kernel, name, out_shape, flops=0, bytes_accessed=0, limit=VMEM_BYTES, **kw):
    return pl.pallas_call(
        kernel,
        out_shape=out_shape,
        compiler_params=pltpu.CompilerParams(vmem_limit_bytes=limit),
        cost_estimate=pl.CostEstimate(
            flops=flops, bytes_accessed=bytes_accessed, transcendentals=0
        ),
        name=name,
        **kw,
    )


def dot_nt(a, b):
    return lax.dot_general(a, b, (((1,), (1,)), ((), ())), preferred_element_type=jnp.float32)


def count_half_rows(rows):
    return max(16, rows // 2)


def gate(wanted):
    wanted = jnp.broadcast_to(wanted, (1, BLOCK))
    return wanted.astype(jnp.float32).astype(jnp.bfloat16)


def take(frames_ref, block):
    return frames_ref[:, pl.ds(pl.multiple_of(block * BLOCK, BLOCK), BLOCK)]


def fold(block, right):
    rows = block.shape[0] // 2
    half = BLOCK // 2
    early, late = block[0:rows].astype(jnp.float32), block[rows:].astype(jnp.float32)
    left = lax.broadcasted_iota(jnp.int32, (rows, BLOCK), 1) < half
    if right:
        folded = jnp.where(left, pltpu.roll(early, half, 1), late)
    else:
        folded = jnp.where(left, early, pltpu.roll(late, half, 1))
    spare = count_half_rows(block.shape[0]) - rows
    if spare:
        folded = jnp.concatenate([folded, jnp.zeros((spare, BLOCK), jnp.float32)])
    return folded.astype(jnp.bfloat16)


def unfold(folded, rows):
    half = BLOCK // 2
    early = folded[0 : rows // 2].astype(jnp.float32)
    left = lax.broadcasted_iota(jnp.int32, early.shape, 1) < half
    return jnp.where(left, early, 0.0), jnp.where(left, pltpu.roll(early, half, 1), 0.0)


def find_members(cm):
    blocks = cm.shape[0]
    first = cm[:, 0:1]
    member = first == lax.broadcasted_iota(jnp.int32, (blocks, BLOCK), 1)
    row = lax.broadcasted_iota(jnp.int32, (blocks, blocks), 0)
    col = lax.broadcasted_iota(jnp.int32, (blocks, blocks), 1)
    earlier = (col < row).astype(jnp.float32).astype(jnp.bfloat16)
    pixels = jnp.sum((cm >= 0).astype(jnp.float32), axis=1, keepdims=True)
    return first, member.astype(jnp.float32), earlier, pixels


def sum_before(earlier, member, values):
    before = jnp.dot(
        earlier, (member * values).astype(jnp.bfloat16), preferred_element_type=jnp.float32
    )
    return jnp.sum(before * member, axis=1, keepdims=True)


def find_blocks(cm, cap_blocks, meta_ref):
    blocks = cm.shape[0]
    width = meta_ref.shape[1]
    first, member, earlier, pixels = find_members(cm)
    rank = sum_before(earlier, member, 1.0).astype(jnp.int32)
    slot = jnp.where(first >= 0, first * cap_blocks + rank, -1)
    hit = slot == lax.broadcasted_iota(jnp.int32, (blocks, width), 1)
    index = lax.broadcasted_iota(jnp.int32, (blocks, width), 0).astype(jnp.float32)
    meta_ref[...] = jnp.zeros_like(meta_ref)
    meta_ref[LIST : LIST + 1, :] = jnp.sum(
        jnp.where(hit, index, 0.0), axis=0, keepdims=True
    ).astype(jnp.int32)
    meta_ref[COUNT : COUNT + 1, 0:BLOCK] = jnp.sum(member, axis=0, keepdims=True).astype(
        jnp.int32
    )
    meta_ref[PIXELS : PIXELS + 1, 0:BLOCK] = jnp.sum(
        member * pixels, axis=0, keepdims=True
    ).astype(jnp.int32)


def find_places(cm):
    _, member, earlier, pixels = find_members(cm)
    valid = (cm >= 0).astype(jnp.float32)
    row = lax.broadcasted_iota(jnp.int32, (BLOCK, BLOCK), 0)
    col = lax.broadcasted_iota(jnp.int32, (BLOCK, BLOCK), 1)
    before = (row < col).astype(jnp.float32).astype(jnp.bfloat16)
    place = jnp.dot(valid.astype(jnp.bfloat16), before, preferred_element_type=jnp.float32)
    return jnp.where(cm >= 0, place + sum_before(earlier, member, pixels), -1.0)


def move_kernel(cap_blocks, cm_hbm, frames_hbm, out_ref, meta_ref, *scratch):
    frames_ref, cm_ref, meta_s, sems = scratch
    n = out_ref.shape[0]
    rows = frames_ref.shape[0]
    kept = cap_blocks // 2
    get_cm = pltpu.make_async_copy(cm_hbm, cm_ref, sems.at[0])
    get_cm.start()
    get_frames = pltpu.make_async_copy(frames_hbm, frames_ref, sems.at[1])
    get_frames.start()
    get_cm.wait()
    find_blocks(cm_ref[...], cap_blocks, meta_ref)
    to_scalars = pltpu.make_async_copy(meta_ref, meta_s, sems.at[2])
    to_scalars.start()
    to_scalars.wait()
    get_frames.wait()
    for q in range(n):
        for i in range(kept + 1, cap_blocks):
            block = meta_s[LIST, q * cap_blocks + i]
            start = (i - kept - 1) * rows
            out_ref[q, start : start + rows] = take(frames_ref, block)
        start = (cap_blocks - kept - 1) * rows
        block = meta_s[LIST, q * cap_blocks + kept]
        out_ref[q, start:] = fold(take(frames_ref, block), True)


def pack_move(cm, frames, cap_blocks):
    rows = frames.shape[0]
    n = cm.shape[0] // cap_blocks
    height = (cap_blocks - cap_blocks // 2 - 1) * rows + count_half_rows(rows)
    meta = jax.ShapeDtypeStruct((8, cm.shape[0]), jnp.int32)
    return call(
        functools.partial(move_kernel, cap_blocks),
        "pack_move",
        [jax.ShapeDtypeStruct((n, height, BLOCK), frames.dtype), meta],
        in_specs=[ANYWHERE] * 2,
        out_specs=[WHOLE] * 2,
        scratch_shapes=[
            pltpu.VMEM(frames.shape, frames.dtype),
            pltpu.VMEM(cm.shape, cm.dtype),
            pltpu.SMEM(meta.shape, meta.dtype),
            pltpu.SemaphoreType.DMA((3,)),
        ],
    )(
        pltpu.with_memory_space_constraint(cm, pltpu.HBM),
        pltpu.with_memory_space_constraint(frames, pltpu.HBM),
    )


def own_kernel(cap_blocks, meta_s, cm_ref, frames_ref, out_hbm, head_ref, *scratch):
    tail_ref, place_ref, sem = scratch
    n, rows, _ = head_ref.shape
    kept = cap_blocks // 2
    for q in range(n):
        for i in range(1, kept):
            block = meta_s[LIST, q * cap_blocks + i]
            tail_ref[q, (i - 1) * rows : i * rows] = take(frames_ref, block)
        block = meta_s[LIST, q * cap_blocks + kept]
        tail_ref[q, (kept - 1) * rows :] = fold(take(frames_ref, block), False)
    write = pltpu.make_async_copy(tail_ref, out_hbm.at[:, rows:], sem)
    write.start()
    place_ref[...] = find_places(cm_ref[...])
    target = lax.broadcasted_iota(jnp.int32, (BLOCK, BLOCK), 0).astype(jnp.float32)
    for q in range(n):
        count, pixels = meta_s[COUNT, q], meta_s[PIXELS, q]
        full = gate(pixels == cap_blocks * BLOCK)
        fits = (pixels <= BLOCK) & (count <= MERGED)
        compact = 0.0
        for i in range(MERGED):
            block = meta_s[LIST, q * cap_blocks + i]
            place = jnp.where(fits & (i < count), place_ref[pl.ds(block, 1), :], -1.0)
            chosen = (target == place).astype(jnp.float32).astype(jnp.bfloat16)
            compact = compact + dot_nt(take(frames_ref, block), chosen)
        block = meta_s[LIST, q * cap_blocks]
        head_ref[q] = compact.astype(jnp.bfloat16) + take(frames_ref, block) * full
    write.wait()


def pack_own(meta, cm, frames, cap_blocks):
    rows = frames.shape[0]
    n = cm.shape[0] // cap_blocks
    tail = (cap_blocks // 2 - 1) * rows + count_half_rows(rows)
    return call(
        functools.partial(own_kernel, cap_blocks),
        "pack_own",
        [
            pltpu.HBM((n, rows + tail, BLOCK), frames.dtype),
            jax.ShapeDtypeStruct((n, rows, BLOCK), frames.dtype),
        ],
        in_specs=[pl.BlockSpec(memory_space=pltpu.SMEM)] + [WHOLE] * 2,
        out_specs=[ANYWHERE, WHOLE],
        scratch_shapes=[
            pltpu.VMEM((n, tail, BLOCK), frames.dtype),
            pltpu.VMEM(cm.shape, jnp.float32),
            pltpu.SemaphoreType.DMA,
        ],
        bytes_accessed=4 * 1024 * 1024,
    )(meta, cm, frames)


def share_kernel(cap_blocks, meta_ref, head_ref, theirs_ref, _, out_hbm, sems, head_sem):
    n, height, _ = out_hbm.shape
    rows = head_ref.shape[1]
    head = pltpu.make_async_copy(head_ref, out_hbm.at[:, 0:rows], head_sem)
    head.start()
    lane = lax.broadcasted_iota(jnp.int32, (1, BLOCK), 1)
    helped = meta_ref[PIXELS : PIXELS + 1, 0:BLOCK] != cap_blocks * BLOCK
    masks = []
    for base in range(0, n, BITS):
        inside = helped & (lane >= base) & (lane < base + BITS)
        bits = jnp.left_shift(1, jnp.clip(lane - base, 0, BITS - 1))
        masks.append(jnp.sum(jnp.where(inside, bits, 0).astype(jnp.float32)).astype(jnp.int32))

    def copies(act):
        for q in range(n):

            @pl.when((masks[q // BITS] >> (q % BITS)) & 1 == 1)
            def _():
                act(
                    pltpu.make_async_copy(
                        theirs_ref.at[q], out_hbm.at[q, rows:height], sems.at[q]
                    )
                )

    copies(lambda copy: copy.start())
    copies(lambda copy: copy.wait())
    head.wait()


def share(meta, own, head, theirs, cap_blocks):
    return call(
        functools.partial(share_kernel, cap_blocks),
        "share",
        pltpu.HBM(own.shape, own.dtype),
        in_specs=[WHOLE] * 3 + [ANYWHERE],
        out_specs=ANYWHERE,
        input_output_aliases={3: 0},
        scratch_shapes=[pltpu.SemaphoreType.DMA((own.shape[0],)), pltpu.SemaphoreType.DMA],
        bytes_accessed=4 * 1024 * 1024,
    )(meta, head, theirs, own)


def left_out(meta, their_meta, cap):
    mine, theirs = meta[PIXELS] == cap, their_meta[PIXELS] == cap
    fits = (meta[PIXELS] <= BLOCK) & (meta[COUNT] <= MERGED)
    return jnp.logical_not(mine | fits), mine & theirs


def rest_kernel(cap_blocks, meta_s, their_meta_s, frames_hbm, cm_hbm, out_ref, *scratch):
    frames_ref, cm_ref = scratch
    n, _, rows, _ = out_ref.shape
    kept = cap_blocks // 2
    pltpu.sync_copy(frames_hbm, frames_ref)
    pltpu.sync_copy(cm_hbm, cm_ref)
    right = lax.broadcasted_iota(jnp.int32, (1, BLOCK), 1) >= BLOCK // 2
    for q in range(n):
        counts = [[ref[row, q] for row in range(PIXELS + 1)] for ref in (meta_s, their_meta_s)]
        large, twice = left_out(*counts, cap_blocks * BLOCK)
        for i in range(cap_blocks):
            block = meta_s[LIST, q * cap_blocks + i]
            wanted = jnp.broadcast_to(large, (1, BLOCK))
            if i >= kept:
                wanted |= twice & right if i == kept else twice
            valid = (cm_ref[pl.ds(block, 1), :] >= 0) & (i < meta_s[COUNT, q])
            out_ref[q, i] = take(frames_ref, block) * gate(valid & wanted)


def pack_rest(meta, their_meta, frames, cm, cap_blocks):
    n = cm.shape[0] // cap_blocks
    return call(
        functools.partial(rest_kernel, cap_blocks),
        "pack_rest",
        jax.ShapeDtypeStruct((n, cap_blocks, frames.shape[0], BLOCK), frames.dtype),
        in_specs=[pl.BlockSpec(memory_space=pltpu.SMEM)] * 2 + [ANYWHERE] * 2,
        out_specs=WHOLE,
        scratch_shapes=[
            pltpu.VMEM(frames.shape, frames.dtype),
            pltpu.VMEM(cm.shape, cm.dtype),
        ],
    )(
        meta,
        their_meta,
        pltpu.with_memory_space_constraint(frames, pltpu.HBM),
        pltpu.with_memory_space_constraint(cm, pltpu.HBM),
    )


def lay_out(raw_ref, rows, first, padded):
    n, height, _ = raw_ref.shape
    total = n * rows
    zero = jnp.zeros((PAD, BLOCK), jnp.float32)
    for i in range(padded.shape[0]):
        slot = first + i
        padded[i, 0:PAD] = zero
        padded[i, PAD + total : 2 * PAD + total] = zero
        for source in range(n):
            start = PAD + source * rows
            if (slot + 1) * rows <= height:
                block = raw_ref[source, slot * rows : (slot + 1) * rows]
                padded[i, start : start + rows] = block.astype(jnp.float32)
            else:
                early, late = unfold(raw_ref[source, slot * rows : height], rows)
                padded[i, start : start + rows // 2] = early
                padded[i, start + rows // 2 : start + rows] = late


def norm_rows(padded, start, chunk, out_ref):
    total = out_ref.shape[0]
    base = PAD + start
    for slot in range(padded.shape[0]):
        raw = padded[slot, base : base + chunk]
        summed = raw
        for offset in range(1, HALF_WIN + 1):
            summed = summed + padded[slot, base - offset : base - offset + chunk]
            summed = summed + padded[slot, base + offset : base + offset + chunk]
        if start == 0 or start + chunk == total:
            frame = start + lax.broadcasted_iota(jnp.int32, (chunk, BLOCK), 0)
            upper = jnp.minimum(frame + HALF_WIN, total - 1)
            lower = jnp.maximum(frame - HALF_WIN, 0)
            mean = summed / (upper - lower + 1).astype(jnp.float32)
        else:
            mean = summed * (1.0 / (2 * HALF_WIN + 1))
        normed = jnp.where(summed > 0.0, raw / mean, 0.0)
        out_ref[start : start + chunk, slot * BLOCK : (slot + 1) * BLOCK] = normed.astype(
            jnp.bfloat16
        )


def norm_kernel(rows, first, raw_ref, *refs):
    out_ref, padded = refs[-2:]
    lay_out(raw_ref, rows, first, padded)
    for start in range(0, out_ref.shape[0], CHUNK):
        norm_rows(padded, start, CHUNK, out_ref)


def normalise(raw, total, first, slots, after=()):
    return call(
        functools.partial(norm_kernel, total // raw.shape[0], first),
        "normalise",
        jax.ShapeDtypeStruct((total, slots * BLOCK), jnp.bfloat16),
        flops=12 * total * slots * BLOCK,
        bytes_accessed=4 * total * slots * BLOCK,
        in_specs=[WHOLE] + [ANYWHERE] * len(after),
        out_specs=WHOLE,
        scratch_shapes=[pltpu.VMEM((slots, total + 2 * PAD, BLOCK), jnp.float32)],
    )(raw, *after)


def set_left(ref, left_ref):
    rows = left_ref.shape[0] - ONES
    first_row = pl.multiple_of(lax.axis_index("pix") * rows, rows)
    left_ref[0:rows] = ref[pl.ds(first_row, rows), :]
    left_ref[rows : rows + ONES] = jnp.ones((ONES, ref.shape[1]), jnp.bfloat16)


def add_sums(pairs, sums, column):
    gram, frame = sums
    rows = pairs[0][0].shape[0] - ONES
    for left_ref, ref in pairs:
        both = dot_nt(left_ref[...], ref[column, :])
        gram = gram + both[0:rows]
        frame = frame + both[rows : rows + 8]
    return gram, frame


def partial_kernel(count, *refs):
    normed, lefts, (gram_out, frame_out) = refs[:count], refs[-count:], refs[-count - 2 : -count]
    before = refs[count : -count - 2]
    for ref, left_ref in zip(normed, lefts):
        set_left(ref, left_ref)
    for start in range(0, gram_out.shape[1], TILE):
        column = slice(start, start + TILE)
        sums = [ref[:, column] for ref in before] or [0.0, 0.0]
        gram_out[:, column], frame_out[:, column] = add_sums(
            list(zip(lefts, normed)), sums, column
        )


def sums_shape(total, parts):
    return [
        jax.ShapeDtypeStruct((total // parts, total), jnp.float32),
        jax.ShapeDtypeStruct((8, total), jnp.float32),
    ]


def partial_sums(normed, before, parts):
    total, width = normed[0].shape
    rows = total // parts
    return call(
        functools.partial(partial_kernel, len(normed)),
        "partial_sums",
        sums_shape(total, parts),
        flops=2 * rows * total * width * len(normed),
        bytes_accessed=4 * rows * total,
        in_specs=[WHOLE] * (len(normed) + len(before)),
        out_specs=[WHOLE] * 2,
        scratch_shapes=[pltpu.VMEM((rows + ONES, x.shape[1]), x.dtype) for x in normed],
    )(*normed, *before)


def result_kernel(meta_ref, their_meta_ref, normed_ref, gram_in, frame_in, out_hbm, *scratch):
    out_ref, frame_ref, sems = scratch
    rows, total = gram_in.shape
    pixels = meta_ref[PIXELS : PIXELS + 1, 0:BLOCK] + their_meta_ref[PIXELS : PIXELS + 1, 0:BLOCK]
    own = lax.broadcasted_iota(jnp.int32, (1, BLOCK), 1) == lax.axis_index("frame")
    number = jnp.sum(jnp.where(own, pixels, 0).astype(jnp.float32), axis=1, keepdims=True)
    ones = jnp.ones((8, normed_ref.shape[1]), jnp.bfloat16)
    frame_ref[...] = frame_in[...] + dot_nt(ones, normed_ref[...])
    first_row = pl.multiple_of(lax.axis_index("pix") * rows, rows)
    row_sum = jnp.broadcast_to(frame_ref[0:1, pl.ds(first_row, rows)], (BLOCK, rows)).T
    row_inv = 1.0 / row_sum[:, 0:1]
    left = normed_ref[pl.ds(first_row, rows), :]
    copies = []
    for i, start in enumerate(range(0, total, TILE)):
        column = slice(start, start + TILE)
        gram = gram_in[:, column] + dot_nt(left, normed_ref[column, :])
        col_inv = 1.0 / frame_ref[0:1, column]
        result = ((gram * row_inv) * col_inv) * number - 1.0
        out_ref[i] = result.astype(jnp.bfloat16)
        copies.append(
            pltpu.make_async_copy(out_ref.at[i], out_hbm.at[0, :, column], sems.at[i])
        )
        copies[-1].start()
    for copy in copies:
        copy.wait()


def correlate(metas, normed, before):
    rows, total = before[0].shape
    tiles = total // TILE
    return call(
        result_kernel,
        "correlate",
        pltpu.HBM((1, rows, total), jnp.bfloat16),
        flops=2 * rows * total * normed.shape[1],
        bytes_accessed=6 * rows * total,
        in_specs=[WHOLE] * 5,
        out_specs=ANYWHERE,
        scratch_shapes=[
            pltpu.VMEM((tiles, rows, TILE), jnp.bfloat16),
            pltpu.VMEM((8, total), jnp.float32),
            pltpu.SemaphoreType.DMA((tiles,)),
        ],
    )(*metas, normed, *before)


def body(frames, cycle_map):
    rows, p_sec = frames.shape
    n = lax.axis_size("frame")
    parts = lax.axis_size("pix")
    total = n * rows
    cap_blocks = p_sec // n // BLOCK
    slots = cap_blocks // 2 + 1
    early = slots - slots // 2
    cm = cycle_map.reshape(p_sec // BLOCK, BLOCK)

    def swap(x):
        return lax.ppermute(x, "pix", SWAP)

    def send(blocks):
        return lax.all_to_all(blocks, "frame", split_axis=0, concat_axis=0, tiled=True)

    moving, meta = pack_move(cm, frames, cap_blocks)
    theirs = swap(moving)
    packed = share(meta, *pack_own(meta, cm, frames, cap_blocks), theirs, cap_blocks)
    received = send(packed)

    meta, _ = lax.optimization_barrier((meta, packed))
    their_meta = swap(meta)
    cap = cap_blocks * BLOCK
    large, twice = left_out(meta[:, :n], their_meta[:, :n], cap)
    overflow = jnp.any(large | twice | left_out(their_meta[:, :n], meta[:, :n], cap)[0])

    first = normalise(received, total, 0, early, [overflow.astype(jnp.int32).reshape(1)])
    their_first = swap(first)
    last = normalise(received, total, early, slots - early, [first])
    their_last = swap(last)
    sums = partial_sums([first, last], [], parts)
    sums = partial_sums([their_first], sums, parts)

    def spill(frames, cm, meta, their_meta, their_last, *sums):
        rest = send(pack_rest(meta, their_meta, frames, cm, cap_blocks))
        normed = normalise(rest.reshape(n, cap_blocks * rows, BLOCK), total, 0, cap_blocks)
        sums = partial_sums([normed, swap(normed)], sums, parts)
        return correlate([meta, their_meta], their_last, sums)

    def fits(frames, cm, meta, their_meta, their_last, *sums):
        return correlate([meta, their_meta], their_last, sums)

    return lax.cond(overflow, spill, fits, frames, cm, meta, their_meta, their_last, *sums)


def solution(mesh):
    return jax.shard_map(
        body,
        mesh=mesh,
        in_specs=(P("frame", "pix"), P("pix")),
        out_specs=P("frame", "pix", None),
        check_vma=False,
    )
```

profile of v0, /device:TPU:11, one launch (start us, length us, event | category | flops | bytes accessed | tf_op | source)
XLA Modules:
  0.0 48.3 jit_solution(14395888250363012778)
XLA Ops:
  0.0 0.0 copy-start
  0.0 0.0 copy-start.2
  0.0 2.3 %pack_move.1 = (bf16[16,224,128]{2,1,0:T(8,128)(2,1)S(1)}, s32[8,128]{1,0:T(8,128)S(1)}) custom-call(s32[128,128]{1,0:T(8,128)} %bitcast.4, bf16[64,16384]{1,0:T(8,128)(2,1)} %frames_ref.1), custom_call_target="tpu_custom_call" | custom-call | tf_op jit(solution)/shard_map/pack_move/pallas_call | solution.py:155
  2.3 0.7 %collective-permute-start.1 = (bf16[16,224,128]{2,1,0:T(8,128)(2,1)S(1)}, bf16[16,224,128]{2,1,0:T(8,128)(2,1)S(1)}, u32[]{:S(2)}, u32[]{:S(2)}) collective-permute-start(bf16[16,224,128]{2,1,0:T(8,128)(2,1)S(1)} %get-tuple-element.57), channel_id=1, source_target_pairs={{0,1},{1,0},{2,3},{3,2},{4,5},{5,4},{6,7},{7,6},{8,9},{9,8},{10,11... | collective-permute-start | bytes 2752520 | tf_op jit(solution)/shard_map/ppermute | solution.py:481
  3.1 0.0 copy-done
  3.1 0.0 copy-done.2
  3.1 2.9 %pack_own.1 = (bf16[16,288,128]{2,1,0:T(8,128)(2,1)}, bf16[16,64,128]{2,1,0:T(8,128)(2,1)S(1)}) custom-call(s32[8,128]{1,0:T(8,128)S(1)} %get-tuple-element.59.meta_s.meta_ref, s32[128,128]{1,0:T(8,128)S(1)} %bitcast.5, bf16[64,16384]{1,0:T(8,128)(2,1)S(1)} %copy-done), custom_call_target="tpu_custom_call" | custom-call | bytes 4194304 | tf_op jit(solution)/shard_map/pack_own/pallas_call | solution.py:206
  6.0 0.0 collective-permute-done.1.theirs_ref
  6.0 1.2 %share.1 = bf16[16,288,128]{2,1,0:T(8,128)(2,1)} custom-call(s32[8,128]{1,0:T(8,128)S(1)} %get-tuple-element.59.meta_s.meta_ref, bf16[16,64,128]{2,1,0:T(8,128)(2,1)S(1)} %get-tuple-element.56.head_ref, bf16[16,224,128]{2,1,0:T(8,128)(2,1)S(1)} %collective-permute-done.1.theirs_ref, ...), custom_call_target="tpu_custom_call", output_to_operand_aliasing={{}: (3, {})} | custom-call | bytes 4194304 | tf_op jit(solution)/shard_map/share/pallas_call | solution.py:254
  7.2 6.6 %all-to-all-start.1 = ((bf16[16,288,128]{2,1,0:T(8,128)(2,1)}), bf16[16,288,128]{2,1,0:T(8,128)(2,1)S(1)}, u32[]{:S(2)}, u32[]{:S(2)}) async-start(bf16[16,288,128]{2,1,0:T(8,128)(2,1)} %share.1), calls=%async_computation.1 | async-start | bytes 2359296 | tf_op jit(solution)/shard_map/all_to_all | solution.py:484
  13.8 0.4 collective-permute-start.2
  14.2 0.8 %collective-permute-done.2 = s32[8,128]{1,0:T(8,128)S(1)} collective-permute-done((s32[8,128]{1,0:T(8,128)S(1)}, s32[8,128]{1,0:T(8,128)S(1)}, u32[]{:S(2)}, u32[]{:S(2)}) %collective-permute-start.2) | collective-permute-done | bytes 4128 | tf_op jit(solution)/shard_map/ppermute | solution.py:481
  15.1 0.6 %or_reduce_fusion = pred[]{:T(512)} fusion(s32[8,128]{1,0:T(8,128)S(1)} %collective-permute-done.2, s32[8,128]{1,0:T(8,128)S(1)} %get-tuple-element.59.meta_s.meta_ref), kind=kLoop, calls=%fused_computation | loop fusion | flops 255 | bytes 257 | tf_op jit(solution)/shard_map/reduce_or | solution.py:495
  16.4 25.3 %all-to-all-done.1.raw_ref = bf16[16,288,128]{2,1,0:T(8,128)(2,1)S(1)} async-done(((bf16[16,288,128]{2,1,0:T(8,128)(2,1)}), bf16[16,288,128]{2,1,0:T(8,128)(2,1)S(1)}, u32[]{:S(2)}, u32[]{:S(2)}) %all-to-all-start.1) | async-done | bytes 1179680 | tf_op jit(solution)/shard_map/all_to_all | solution.py:484
  41.6 0.6 %normalise.4.refs_0_ = bf16[1024,384]{1,0:T(8,128)(2,1)S(1)} custom-call(bf16[16,288,128]{2,1,0:T(8,128)(2,1)S(1)} %all-to-all-done.1.raw_ref, s32[1]{0:T(128)} %bitcast.2.refs_0_), custom_call_target="tpu_custom_call" | custom-call | flops 4718592 | bytes 1572864 | tf_op jit(solution)/shard_map/normalise/pallas_call | solution.py:360
  42.3 1.6 %collective-permute-start.4 = (bf16[1024,384]{1,0:T(8,128)(2,1)S(1)}, bf16[1024,384]{1,0:T(8,128)(2,1)S(1)}, u32[]{:S(2)}, u32[]{:S(2)}) collective-permute-start(bf16[1024,384]{1,0:T(8,128)(2,1)S(1)} %normalise.4.refs_0_), channel_id=1, source_target_pairs={{0,1},{1,0},{2,3},{3,2},{4,5},{5,4},{6,7},{7,6},{8,9},{9,8},{10,11... | collective-permute-start | bytes 2359304 | tf_op jit(solution)/shard_map/ppermute | solution.py:481
  43.8 0.5 normalise.5.refs_1_
  44.3 0.1 collective-permute-start.3
  44.4 1.0 %partial_sums.4 = (f32[512,1024]{1,0:T(8,128)S(1)}, f32[8,1024]{1,0:T(8,128)S(1)}) custom-call(bf16[1024,384]{1,0:T(8,128)(2,1)S(1)} %normalise.4.refs_0_, bf16[1024,256]{1,0:T(8,128)(2,1)S(1)} %normalise.5.refs_1_), custom_call_target="tpu_custom_call" | custom-call | flops 805306368 | bytes 2097152 | tf_op jit(solution)/shard_map/partial_sums/pallas_call | solution.py:412
  45.4 0.3 collective-permute-done.4.refs_0_
  45.7 0.8 %partial_sums.5 = (f32[512,1024]{1,0:T(8,128)S(1)}, f32[8,1024]{1,0:T(8,128)S(1)}) custom-call(bf16[1024,384]{1,0:T(8,128)(2,1)S(1)} %collective-permute-done.4.refs_0_, f32[512,1024]{1,0:T(8,128)S(1)} %get-tuple-element.60.refs_1_, f32[8,1024]{1,0:T(8,128)S(1)} %get-tuple-element.61.refs_2_), custom_call_target="tpu_custom_call" | custom-call | flops 402653184 | bytes 2097152 | tf_op jit(solution)/shard_map/partial_sums/pallas_call | solution.py:412
  46.5 0.0 collective-permute-done.3
  46.5 1.8 %conditional.1 = (bf16[1,512,1024]{2,1,0:T(8,128)(2,1)}) conditional(s32[]{:T(128)} %convert_element_type.4, (s32[8,128]{1,0:T(8,128)S(1)}, s32[8,128]{1,0:T(8,128)S(1)}, bf16[1024,256]{1,0:T(8,128)(2,1)S(1)}, f32[512,1024]{1,0:T(8,128)S(1)}, f32[8,1024]{1,0:T(8,128)S(1)}) %tuple.13, (s32[8,128]{1,0:T(8,128)S(1)}, s32[8,128]{1,0:T(8,128)S(1)}, ...), branch_computations={%region_1.0_spmd, %region_2.0_spmd} | conditional | flops 2428502016 | bytes 30670952 | solution.py:513
  46.5 1.8 %correlate.2 = bf16[1,512,1024]{2,1,0:T(8,128)(2,1)} custom-call(s32[8,128]{1,0:T(8,128)S(1)} %get-tuple-element.32.meta_ref, s32[8,128]{1,0:T(8,128)S(1)} %get-tuple-element.33.their_meta_ref, bf16[1024,256]{1,0:T(8,128)(2,1)S(1)} %get-tuple-element.34.normed_ref, f32[512,1024]{1,0:T(8,128)S(1)} %get-tuple-element.35.gram_in, ...), custom_call_target="tpu_custom_call" | custom-call | flops 268435456 | bytes 3145728 | tf_op jit(solution)/shard_map/cond/branch_0_fun/correlate/pallas_call | solution.py:454
Async XLA Ops:
  0.0 3.1 %copy-start = (bf16[64,16384]{1,0:T(8,128)(2,1)S(1)}, bf16[64,16384]{1,0:T(8,128)(2,1)}, u32[]{:S(2)}) copy-start(bf16[64,16384]{1,0:T(8,128)(2,1)} %frames_ref.1) | copy-start | bytes 6291460
  0.0 3.1 %copy-start.2 = (s32[16384]{0:T(1024)S(1)}, s32[16384]{0:T(1024)}, u32[]{:S(2)}) copy-start(s32[16384]{0:T(1024)} %param.5) | copy-start | bytes 196612
  2.3 3.6 %collective-permute-start.1 = (bf16[16,224,128]{2,1,0:T(8,128)(2,1)S(1)}, bf16[16,224,128]{2,1,0:T(8,128)(2,1)S(1)}, u32[]{:S(2)}, u32[]{:S(2)}) collective-permute-start(bf16[16,224,128]{2,1,0:T(8,128)(2,1)S(1)} %get-tuple-element.57), channel_id=1, source_target_pairs={{0,1},{1,0},{2,3},{3,2},{4,5},{5,4},{6,7},{7,6},{8,9},{9,8},{10,11... | collective-permute-start | bytes 2752520 | tf_op jit(solution)/shard_map/ppermute | solution.py:481
  7.2 34.5 %all-to-all-start.1 = ((bf16[16,288,128]{2,1,0:T(8,128)(2,1)}), bf16[16,288,128]{2,1,0:T(8,128)(2,1)S(1)}, u32[]{:S(2)}, u32[]{:S(2)}) async-start(bf16[16,288,128]{2,1,0:T(8,128)(2,1)} %share.1), calls=%async_computation.1 | async-start | bytes 2359296 | tf_op jit(solution)/shard_map/all_to_all | solution.py:484
  13.8 1.3 %collective-permute-start.2 = (s32[8,128]{1,0:T(8,128)S(1)}, s32[8,128]{1,0:T(8,128)S(1)}, u32[]{:S(2)}, u32[]{:S(2)}) collective-permute-start(s32[8,128]{1,0:T(8,128)S(1)} %get-tuple-element.59.meta_s.meta_ref), channel_id=1, source_target_pairs={{0,1},{1,0},{2,3},{3,2},{4,5},{5,4},{6,7},{7,6},{8,9},{9,8},{10,11... | collective-permute-start | bytes 12296 | tf_op jit(solution)/shard_map/ppermute | solution.py:481
  42.3 3.5 %collective-permute-start.4 = (bf16[1024,384]{1,0:T(8,128)(2,1)S(1)}, bf16[1024,384]{1,0:T(8,128)(2,1)S(1)}, u32[]{:S(2)}, u32[]{:S(2)}) collective-permute-start(bf16[1024,384]{1,0:T(8,128)(2,1)S(1)} %normalise.4.refs_0_), channel_id=1, source_target_pairs={{0,1},{1,0},{2,3},{3,2},{4,5},{5,4},{6,7},{7,6},{8,9},{9,8},{10,11... | collective-permute-start | bytes 2359304 | tf_op jit(solution)/shard_map/ppermute | solution.py:481
  44.3 2.2 %collective-permute-start.3 = (bf16[1024,256]{1,0:T(8,128)(2,1)S(1)}, bf16[1024,256]{1,0:T(8,128)(2,1)S(1)}, u32[]{:S(2)}, u32[]{:S(2)}) collective-permute-start(bf16[1024,256]{1,0:T(8,128)(2,1)S(1)} %normalise.5.refs_1_), channel_id=1, source_target_pairs={{0,1},{1,0},{2,3},{3,2},{4,5},{5,4},{6,7},{7,6},{8,9},{9,8},{10,11... | collective-permute-start | bytes 1572872 | tf_op jit(solution)/shard_map/ppermute | solution.py:481
where the time goes:
time: 48.8 us; the launch traced here: 48.3 us
  waiting for transfers between devices  26.4 us (54%)
  Pallas kernels  11.1 us (23%)
  starting transfers between devices  9.46 us (19%)
  between operations  0.72 us (1%)
  other arithmetic  0.64 us (1%)
    all_to_all x1, waiting for transfers between devices, send(): lax.all_to_all(blocks, 'frame', split_axis=0, concat_axis=0, tiled=True)  25.3 us
    all_to_all x1, starting transfers between devices, send(): lax.all_to_all(blocks, 'frame', split_axis=0, concat_axis=0, tiled=True)  6.65 us
    pallas_call x1, Pallas kernels, pack_own(): call(functools.partial(own_kernel, cap_blocks), 'pack_own', [pltpu.HBM((n...  2.9 us
    ppermute x4, starting transfers between devices, swap(): return lax.ppermute(x, 'pix', SWAP)  2.81 us
    pallas_call x1, Pallas kernels, pack_move(): call(functools.partial(move_kernel, cap_blocks), 'pack_move', [jax.ShapeD...  2.33 us
    pallas_call x2, Pallas kernels, partial_sums(): call(functools.partial(partial_kernel, len(normed)), 'partial_sums', sums...  1.81 us
    pallas_call x1, Pallas kernels, correlate(): call(result_kernel, 'correlate', pltpu.HBM((1, rows, total), jnp.bfloat16...  1.75 us
    pallas_call x1, Pallas kernels, share(): call(functools.partial(share_kernel, cap_blocks), 'share', pltpu.HBM(own....  1.16 us
  transfers between devices with their start and end apart: 5, of which 3 were waited for; matrix products, arithmetic and copies ran while one was open for 1% of the time, Pallas kernels for 11%

commit v1 on v0

--- a/solution.py
+++ b/solution.py
@@ -171,19 +171,12 @@
 
 
 def own_kernel(cap_blocks, meta_s, cm_ref, frames_ref, out_hbm, head_ref, *scratch):
-    tail_ref, place_ref, sem = scratch
+    tail_ref, place_ref, sems = scratch
     n, rows, _ = head_ref.shape
     kept = cap_blocks // 2
-    for q in range(n):
-        for i in range(1, kept):
-            block = meta_s[LIST, q * cap_blocks + i]
-            tail_ref[q, (i - 1) * rows : i * rows] = take(frames_ref, block)
-        block = meta_s[LIST, q * cap_blocks + kept]
-        tail_ref[q, (kept - 1) * rows :] = fold(take(frames_ref, block), False)
-    write = pltpu.make_async_copy(tail_ref, out_hbm.at[:, rows:], sem)
-    write.start()
     place_ref[...] = find_places(cm_ref[...])
     target = lax.broadcasted_iota(jnp.int32, (BLOCK, BLOCK), 0).astype(jnp.float32)
+    writes = []
     for q in range(n):
         count, pixels = meta_s[COUNT, q], meta_s[PIXELS, q]
         full = gate(pixels == cap_blocks * BLOCK)
@@ -196,7 +189,21 @@
             compact = compact + dot_nt(take(frames_ref, block), chosen)
         block = meta_s[LIST, q * cap_blocks]
         head_ref[q] = compact.astype(jnp.bfloat16) + take(frames_ref, block) * full
-    write.wait()
+        for i in range(1, kept):
+            block = meta_s[LIST, q * cap_blocks + i]
+            tail_ref[q, (i - 1) * rows : i * rows] = take(frames_ref, block)
+        block = meta_s[LIST, q * cap_blocks + kept]
+        tail_ref[q, (kept - 1) * rows :] = fold(take(frames_ref, block), False)
+        if q + 1 in (n * 3 // 4, n):
+            part = pl.ds(0, n * 3 // 4) if q + 1 < n else pl.ds(n * 3 // 4, n - n * 3 // 4)
+            writes.append(
+                pltpu.make_async_copy(
+                    tail_ref.at[part], out_hbm.at[part, rows:], sems.at[len(writes)]
+                )
+            )
+            writes[-1].start()
+    for write in writes:
+        write.wait()
 
 
 def pack_own(meta, cm, frames, cap_blocks):
@@ -215,7 +222,7 @@
         scratch_shapes=[
             pltpu.VMEM((n, tail, BLOCK), frames.dtype),
             pltpu.VMEM(cm.shape, jnp.float32),
-            pltpu.SemaphoreType.DMA,
+            pltpu.SemaphoreType.DMA((2,)),
         ],
         bytes_accessed=4 * 1024 * 1024,
     )(meta, cm, frames)

time: 48.8 us -> 48.8 us (level)
  no operation moved by 1% of the time
where the time goes in v1:
time: 48.8 us; the launch traced here: 48.2 us
  waiting for transfers between devices  26.5 us (54%)
  Pallas kernels  11 us (23%)
  starting transfers between devices  9.26 us (19%)
  between operations  0.72 us (1%)
  other arithmetic  0.64 us (1%)
    all_to_all x1, waiting for transfers between devices, send(): lax.all_to_all(blocks, 'frame', split_axis=0, concat_axis=0, tiled=True)  25.4 us
    all_to_all x1, starting transfers between devices, send(): lax.all_to_all(blocks, 'frame', split_axis=0, concat_axis=0, tiled=True)  6.68 us
    pallas_call x1, Pallas kernels, pack_own(): call(functools.partial(own_kernel, cap_blocks), 'pack_own', [pltpu.HBM((n...  2.86 us
    ppermute x4, starting transfers between devices, swap(): return lax.ppermute(x, 'pix', SWAP)  2.59 us
    pallas_call x1, Pallas kernels, pack_move(): call(functools.partial(move_kernel, cap_blocks), 'pack_move', [jax.ShapeD...  2.33 us
    pallas_call x2, Pallas kernels, partial_sums(): call(functools.partial(partial_kernel, len(normed)), 'partial_sums', sums...  1.81 us
    pallas_call x1, Pallas kernels, correlate(): call(result_kernel, 'correlate', pltpu.HBM((1, rows, total), jnp.bfloat16...  1.75 us
    pallas_call x1, Pallas kernels, share(): call(functools.partial(share_kernel, cap_blocks), 'share', pltpu.HBM(own....  1.17 us
  transfers between devices with their start and end apart: 5, of which 3 were waited for; matrix products, arithmetic and copies ran while one was open for 1% of the time, Pallas kernels for 11%

profile of v1, /device:TPU:11, one launch (start us, length us, event | category | flops | bytes accessed | tf_op | source)
XLA Modules:
  0.0 48.2 jit_solution(17329294954065124969)
XLA Ops:
  0.0 0.0 copy-start
  0.0 0.0 copy-start.2
  0.0 2.3 %pack_move.1 = (bf16[16,224,128]{2,1,0:T(8,128)(2,1)S(1)}, s32[8,128]{1,0:T(8,128)S(1)}) custom-call(s32[128,128]{1,0:T(8,128)} %bitcast.4, bf16[64,16384]{1,0:T(8,128)(2,1)} %frames_ref.1), custom_call_target="tpu_custom_call" | custom-call | tf_op jit(solution)/shard_map/pack_move/pallas_call | solution.py:155
  2.3 0.7 %collective-permute-start.1 = (bf16[16,224,128]{2,1,0:T(8,128)(2,1)S(1)}, bf16[16,224,128]{2,1,0:T(8,128)(2,1)S(1)}, u32[]{:S(2)}, u32[]{:S(2)}) collective-permute-start(bf16[16,224,128]{2,1,0:T(8,128)(2,1)S(1)} %get-tuple-element.57), channel_id=1, source_target_pairs={{0,1},{1,0},{2,3},{3,2},{4,5},{5,4},{6,7},{7,6},{8,9},{9,8},{10,11... | collective-permute-start | bytes 2752520 | tf_op jit(solution)/shard_map/ppermute | solution.py:488
  3.1 0.0 copy-done
  3.1 0.0 copy-done.2
  3.1 2.9 %pack_own.1 = (bf16[16,288,128]{2,1,0:T(8,128)(2,1)}, bf16[16,64,128]{2,1,0:T(8,128)(2,1)S(1)}) custom-call(s32[8,128]{1,0:T(8,128)S(1)} %get-tuple-element.59.meta_s.meta_ref, s32[128,128]{1,0:T(8,128)S(1)} %bitcast.5, bf16[64,16384]{1,0:T(8,128)(2,1)S(1)} %copy-done), custom_call_target="tpu_custom_call" | custom-call | bytes 4194304 | tf_op jit(solution)/shard_map/pack_own/pallas_call | solution.py:213
  5.9 0.0 collective-permute-done.1.theirs_ref
  6.0 1.2 %share.1 = bf16[16,288,128]{2,1,0:T(8,128)(2,1)} custom-call(s32[8,128]{1,0:T(8,128)S(1)} %get-tuple-element.59.meta_s.meta_ref, bf16[16,64,128]{2,1,0:T(8,128)(2,1)S(1)} %get-tuple-element.56.head_ref, bf16[16,224,128]{2,1,0:T(8,128)(2,1)S(1)} %collective-permute-done.1.theirs_ref, ...), custom_call_target="tpu_custom_call", output_to_operand_aliasing={{}: (3, {})} | custom-call | bytes 4194304 | tf_op jit(solution)/shard_map/share/pallas_call | solution.py:261
  7.1 6.7 %all-to-all-start.1 = ((bf16[16,288,128]{2,1,0:T(8,128)(2,1)}), bf16[16,288,128]{2,1,0:T(8,128)(2,1)S(1)}, u32[]{:S(2)}, u32[]{:S(2)}) async-start(bf16[16,288,128]{2,1,0:T(8,128)(2,1)} %share.1), calls=%async_computation.1 | async-start | bytes 2359296 | tf_op jit(solution)/shard_map/all_to_all | solution.py:491
  13.8 0.4 collective-permute-start.2
  14.2 0.8 %collective-permute-done.2 = s32[8,128]{1,0:T(8,128)S(1)} collective-permute-done((s32[8,128]{1,0:T(8,128)S(1)}, s32[8,128]{1,0:T(8,128)S(1)}, u32[]{:S(2)}, u32[]{:S(2)}) %collective-permute-start.2) | collective-permute-done | bytes 4128 | tf_op jit(solution)/shard_map/ppermute | solution.py:488
  15.0 0.6 %or_reduce_fusion = pred[]{:T(512)} fusion(s32[8,128]{1,0:T(8,128)S(1)} %collective-permute-done.2, s32[8,128]{1,0:T(8,128)S(1)} %get-tuple-element.59.meta_s.meta_ref), kind=kLoop, calls=%fused_computation | loop fusion | flops 255 | bytes 257 | tf_op jit(solution)/shard_map/reduce_or | solution.py:502
  16.3 25.4 %all-to-all-done.1.raw_ref = bf16[16,288,128]{2,1,0:T(8,128)(2,1)S(1)} async-done(((bf16[16,288,128]{2,1,0:T(8,128)(2,1)}), bf16[16,288,128]{2,1,0:T(8,128)(2,1)S(1)}, u32[]{:S(2)}, u32[]{:S(2)}) %all-to-all-start.1) | async-done | bytes 1179680 | tf_op jit(solution)/shard_map/all_to_all | solution.py:491
  41.7 0.6 %normalise.4.refs_0_ = bf16[1024,384]{1,0:T(8,128)(2,1)S(1)} custom-call(bf16[16,288,128]{2,1,0:T(8,128)(2,1)S(1)} %all-to-all-done.1.raw_ref, s32[1]{0:T(128)} %bitcast.2.refs_0_), custom_call_target="tpu_custom_call" | custom-call | flops 4718592 | bytes 1572864 | tf_op jit(solution)/shard_map/normalise/pallas_call | solution.py:367
  42.4 1.4 %collective-permute-start.4 = (bf16[1024,384]{1,0:T(8,128)(2,1)S(1)}, bf16[1024,384]{1,0:T(8,128)(2,1)S(1)}, u32[]{:S(2)}, u32[]{:S(2)}) collective-permute-start(bf16[1024,384]{1,0:T(8,128)(2,1)S(1)} %normalise.4.refs_0_), channel_id=1, source_target_pairs={{0,1},{1,0},{2,3},{3,2},{4,5},{5,4},{6,7},{7,6},{8,9},{9,8},{10,11... | collective-permute-start | bytes 2359304 | tf_op jit(solution)/shard_map/ppermute | solution.py:488
  43.8 0.5 normalise.5.refs_1_
  44.2 0.1 collective-permute-start.3
  44.3 1.0 %partial_sums.4 = (f32[512,1024]{1,0:T(8,128)S(1)}, f32[8,1024]{1,0:T(8,128)S(1)}) custom-call(bf16[1024,384]{1,0:T(8,128)(2,1)S(1)} %normalise.4.refs_0_, bf16[1024,256]{1,0:T(8,128)(2,1)S(1)} %normalise.5.refs_1_), custom_call_target="tpu_custom_call" | custom-call | flops 805306368 | bytes 2097152 | tf_op jit(solution)/shard_map/partial_sums/pallas_call | solution.py:419
  45.4 0.3 collective-permute-done.4.refs_0_
  45.7 0.8 %partial_sums.5 = (f32[512,1024]{1,0:T(8,128)S(1)}, f32[8,1024]{1,0:T(8,128)S(1)}) custom-call(bf16[1024,384]{1,0:T(8,128)(2,1)S(1)} %collective-permute-done.4.refs_0_, f32[512,1024]{1,0:T(8,128)S(1)} %get-tuple-element.60.refs_1_, f32[8,1024]{1,0:T(8,128)S(1)} %get-tuple-element.61.refs_2_), custom_call_target="tpu_custom_call" | custom-call | flops 402653184 | bytes 2097152 | tf_op jit(solution)/shard_map/partial_sums/pallas_call | solution.py:419
  46.4 0.0 collective-permute-done.3
  46.5 1.8 %conditional.1 = (bf16[1,512,1024]{2,1,0:T(8,128)(2,1)}) conditional(s32[]{:T(128)} %convert_element_type.4, (s32[8,128]{1,0:T(8,128)S(1)}, s32[8,128]{1,0:T(8,128)S(1)}, bf16[1024,256]{1,0:T(8,128)(2,1)S(1)}, f32[512,1024]{1,0:T(8,128)S(1)}, f32[8,1024]{1,0:T(8,128)S(1)}) %tuple.13, (s32[8,128]{1,0:T(8,128)S(1)}, s32[8,128]{1,0:T(8,128)S(1)}, ...), branch_computations={%region_1.0_spmd, %region_2.0_spmd} | conditional | flops 2428502016 | bytes 30670952 | solution.py:520
  46.5 1.7 %correlate.2 = bf16[1,512,1024]{2,1,0:T(8,128)(2,1)} custom-call(s32[8,128]{1,0:T(8,128)S(1)} %get-tuple-element.32.meta_ref, s32[8,128]{1,0:T(8,128)S(1)} %get-tuple-element.33.their_meta_ref, bf16[1024,256]{1,0:T(8,128)(2,1)S(1)} %get-tuple-element.34.normed_ref, f32[512,1024]{1,0:T(8,128)S(1)} %get-tuple-element.35.gram_in, ...), custom_call_target="tpu_custom_call" | custom-call | flops 268435456 | bytes 3145728 | tf_op jit(solution)/shard_map/cond/branch_0_fun/correlate/pallas_call | solution.py:461
Async XLA Ops:
  0.0 3.1 %copy-start = (bf16[64,16384]{1,0:T(8,128)(2,1)S(1)}, bf16[64,16384]{1,0:T(8,128)(2,1)}, u32[]{:S(2)}) copy-start(bf16[64,16384]{1,0:T(8,128)(2,1)} %frames_ref.1) | copy-start | bytes 6291460
  0.0 3.1 %copy-start.2 = (s32[16384]{0:T(1024)S(1)}, s32[16384]{0:T(1024)}, u32[]{:S(2)}) copy-start(s32[16384]{0:T(1024)} %param.5) | copy-start | bytes 196612
  2.3 3.6 %collective-permute-start.1 = (bf16[16,224,128]{2,1,0:T(8,128)(2,1)S(1)}, bf16[16,224,128]{2,1,0:T(8,128)(2,1)S(1)}, u32[]{:S(2)}, u32[]{:S(2)}) collective-permute-start(bf16[16,224,128]{2,1,0:T(8,128)(2,1)S(1)} %get-tuple-element.57), channel_id=1, source_target_pairs={{0,1},{1,0},{2,3},{3,2},{4,5},{5,4},{6,7},{7,6},{8,9},{9,8},{10,11... | collective-permute-start | bytes 2752520 | tf_op jit(solution)/shard_map/ppermute | solution.py:488
  7.1 34.6 %all-to-all-start.1 = ((bf16[16,288,128]{2,1,0:T(8,128)(2,1)}), bf16[16,288,128]{2,1,0:T(8,128)(2,1)S(1)}, u32[]{:S(2)}, u32[]{:S(2)}) async-start(bf16[16,288,128]{2,1,0:T(8,128)(2,1)} %share.1), calls=%async_computation.1 | async-start | bytes 2359296 | tf_op jit(solution)/shard_map/all_to_all | solution.py:491
  13.8 1.2 %collective-permute-start.2 = (s32[8,128]{1,0:T(8,128)S(1)}, s32[8,128]{1,0:T(8,128)S(1)}, u32[]{:S(2)}, u32[]{:S(2)}) collective-permute-start(s32[8,128]{1,0:T(8,128)S(1)} %get-tuple-element.59.meta_s.meta_ref), channel_id=1, source_target_pairs={{0,1},{1,0},{2,3},{3,2},{4,5},{5,4},{6,7},{7,6},{8,9},{9,8},{10,11... | collective-permute-start | bytes 12296 | tf_op jit(solution)/shard_map/ppermute | solution.py:488
  42.4 3.3 %collective-permute-start.4 = (bf16[1024,384]{1,0:T(8,128)(2,1)S(1)}, bf16[1024,384]{1,0:T(8,128)(2,1)S(1)}, u32[]{:S(2)}, u32[]{:S(2)}) collective-permute-start(bf16[1024,384]{1,0:T(8,128)(2,1)S(1)} %normalise.4.refs_0_), channel_id=1, source_target_pairs={{0,1},{1,0},{2,3},{3,2},{4,5},{5,4},{6,7},{7,6},{8,9},{9,8},{10,11... | collective-permute-start | bytes 2359304 | tf_op jit(solution)/shard_map/ppermute | solution.py:488
  44.2 2.2 %collective-permute-start.3 = (bf16[1024,256]{1,0:T(8,128)(2,1)S(1)}, bf16[1024,256]{1,0:T(8,128)(2,1)S(1)}, u32[]{:S(2)}, u32[]{:S(2)}) collective-permute-start(bf16[1024,256]{1,0:T(8,128)(2,1)S(1)} %normalise.5.refs_1_), channel_id=1, source_target_pairs={{0,1},{1,0},{2,3},{3,2},{4,5},{5,4},{6,7},{7,6},{8,9},{9,8},{10,11... | collective-permute-start | bytes 1572872 | tf_op jit(solution)/shard_map/ppermute | solution.py:488
